TPU v7x, 32 devices: a whole 2x2x4 slice. The times are simulated.
32 devices in a mesh: section: 4 (over x, core), dp: 8 (over z, y).
Axes of the slice: x: 2, y: 2, z: 4, core: 2. Of those that a mesh axis runs over, the one named last changes fastest.
Arguments:
- inputs: bfloat16 [2, 1024, 1536], P(None, 'dp'), may hold values from -6 to 6
- grad_out: bfloat16 [2, 1024, 1536], P(None, 'dp'), may hold values from -6 to 6
- w_conv: bfloat16 [4, 4608, 768], P('section'), may hold values from -0.09375 to 0.09375
- w_point: bfloat16 [4, 768, 1536], P('section'), may hold values from -0.21875 to 0.21875
- gain_conv: float32 [4, 1536], P('section'), may hold values from 0.25 to 1.75
- gain_point: float32 [4, 768], P('section'), may hold values from 0.25 to 1.75
Outputs:
- grad_w_conv: float32 [4, 4608, 768], P('section', 'dp')
- grad_w_point: float32 [4, 768, 1536], P('section', 'dp')
- grad_gain_conv: float32 [4, 1536], P('section', 'dp')
- grad_gain_point: float32 [4, 768], P('section', 'dp')
- grad_acts: bfloat16 [4, 2, 1024, 1536], P('section', None, 'dp')
All inputs are finite; a program needn't handle non-finite values.
Results may differ from a plain program's by a relative error of at most 0.034.
Values may be sent and summed in bfloat16 or wider, within the bound.
A program may use at most 128 MiB of HBM per device.

v0:
```python
import functools
import math

import jax
import jax.numpy as jnp
from jax import lax
from jax.experimental import pallas as pl
from jax.experimental.pallas import tpu as pltpu
from jax.sharding import PartitionSpec as P

EPSILON = 1e-06
MESH = pl.DeviceIdType.MESH
GELU_C = math.sqrt(2.0 / math.pi)


def normed(values):
    mean_sq = jnp.mean(values * values, axis=-1, keepdims=True)
    rate = lax.rsqrt(mean_sq + EPSILON)
    return values * rate, rate


def gelu(u):
    return 0.5 * u * (1.0 + jnp.tanh(GELU_C * (u + 0.044715 * u * u * u)))


def act_pull(values, gain, upstream):
    unit, rate = normed(values)
    u = unit * gain
    square = u * u
    bent = jnp.tanh(GELU_C * (u + 0.044715 * square * u))
    slope = 0.5 * (1.0 + bent) + 0.5 * u * (1.0 - bent * bent) * GELU_C * (
        1.0 + 3.0 * 0.044715 * square
    )
    inner = upstream * slope
    grad_gain = jnp.sum(inner * unit, axis=0, keepdims=True)
    scaled = inner * gain
    drift = jnp.mean(scaled * unit, axis=-1, keepdims=True)
    return rate * (scaled - unit * drift), grad_gain


def dot(left, right):
    return jnp.dot(left, right, preferred_element_type=jnp.float32)


def dot_nt(left, right):
    return lax.dot_general(
        left, right, (((1,), (1,)), ((), ())), preferred_element_type=jnp.float32
    )


def dot_tn(left, right):
    return lax.dot_general(
        left, right, (((0,), (0,)), ((), ())), preferred_element_type=jnp.float32
    )


def pick(rows, source_rows, offset):
    row = lax.broadcasted_iota(jnp.int32, (rows, source_rows), 0)
    column = lax.broadcasted_iota(jnp.int32, (rows, source_rows), 1)
    return jnp.where(column - row == offset, 1.0, 0.0).astype(jnp.bfloat16)


def window(share):
    most = max((share * j) % 128 for j in range(128))
    return -(-(share + most) // 128) * 128


def tower(
    sections, group, halo,
    inputs, grad_out, w_conv, w_point, gain_conv, gain_point,
    grads, acts_all, q_all, point_all, gains_all,
    h_in, h_out, e_in, conv, mix, columns, q_own, halo_a, halo_q, point_sum, point_own, gains,
    sec_send, sec_recv, halo_send, halo_recv,
    acts_send, acts_recv, q_send, q_recv, point_send, point_recv, gains_send, gains_recv, own_sem,
):
    section = lax.axis_index("section")
    me = lax.axis_index("dp")
    micros, positions, channels = inputs.shape
    inner = w_conv.shape[1]
    share = 3 * channels // group
    wide = window(share)
    first, last = section == 0, section == sections - 1
    left_end, right_end = me == 0, me == group - 1

    dilation = jnp.int32(1)
    for index in range(sections):
        dilation = jnp.where(section == index, 3**index // 2**index, dilation)

    halo_a[...] = jnp.zeros_like(halo_a)
    halo_q[...] = jnp.zeros_like(halo_q)
    gains[...] = jnp.zeros_like(gains)
    point_sum[...] = jnp.zeros_like(point_sum)

    barrier = pltpu.get_barrier_semaphore()

    def greet(off, carry):
        pl.semaphore_signal(
            barrier, inc=1, device_id={"dp": lax.rem(me + off, group)}, device_id_type=MESH
        )
        return carry

    lax.fori_loop(1, group, greet, 0)

    @pl.when(jnp.logical_not(first))
    def _():
        pl.semaphore_signal(barrier, inc=1, device_id={"section": section - 1}, device_id_type=MESH)

    @pl.when(jnp.logical_not(last))
    def _():
        pl.semaphore_signal(barrier, inc=1, device_id={"section": section + 1}, device_id_type=MESH)

    beside = jnp.where(first, 0, 1) + jnp.where(last, 0, 1)
    pl.semaphore_wait(barrier, group - 1 + beside)

    def remote(src, dst, send, recv, device):
        return pltpu.make_async_remote_copy(
            src_ref=src, dst_ref=dst, send_sem=send, recv_sem=recv,
            device_id=device, device_id_type=MESH,
        )

    def forward_copy(m):
        return remote(
            h_out.at[m], h_in.at[m], sec_send.at[0, m], sec_recv.at[0, m], {"section": section + 1}
        )

    def backward_copy(m):
        return remote(
            grads.at[m], e_in.at[m], sec_send.at[1, m], sec_recv.at[1, m], {"section": section - 1}
        )

    def halo_copy(kind, m, side):
        rows = pl.ds(positions - halo, halo) if side == 0 else pl.ds(0, halo)
        if kind == 0:
            src, store = columns.at[m, rows, pl.ds(channels, channels)], halo_a
        else:
            src, store = q_own.at[m, rows], halo_q
        return remote(
            src, store.at[m, side], halo_send.at[kind, m, side], halo_recv.at[kind, m, side],
            {"dp": me + 1 if side == 0 else me - 1},
        )

    def start_halos(kind, m):
        @pl.when(jnp.logical_not(right_end))
        def _():
            halo_copy(kind, m, 0).start()

        @pl.when(jnp.logical_not(left_end))
        def _():
            halo_copy(kind, m, 1).start()

    def wait_halos(kind, m):
        @pl.when(jnp.logical_not(left_end))
        def _():
            halo_copy(kind, m, 0).wait_recv()

        @pl.when(jnp.logical_not(right_end))
        def _():
            halo_copy(kind, m, 1).wait_recv()

    def wait_halo_sends(kind, m):
        @pl.when(jnp.logical_not(right_end))
        def _():
            halo_copy(kind, m, 0).wait_send()

        @pl.when(jnp.logical_not(left_end))
        def _():
            halo_copy(kind, m, 1).wait_send()

    def acts_part(m, owner):
        start = pl.multiple_of((share * owner) // 128 * 128, 128)
        return columns.at[m, :, pl.ds(start, wide)]

    def acts_copy(m, off):
        peer = lax.rem(me + off, group)
        return remote(
            acts_part(m, peer), acts_all.at[me, m], acts_send.at[m, off], acts_recv.at[m, off],
            {"dp": peer},
        )

    def q_copy(m, off):
        peer = lax.rem(me + off, group)
        return remote(
            q_own.at[m], q_all.at[me, m], q_send.at[m, off], q_recv.at[m, off], {"dp": peer}
        )

    def point_copy(off):
        peer = lax.rem(me + off, group)
        return remote(
            point_own.at[peer], point_all.at[me], point_send.at[off], point_recv.at[off],
            {"dp": peer},
        )

    def gains_copy(off):
        peer = lax.rem(me + off, group)
        return remote(
            gains, gains_all.at[me], gains_send.at[off], gains_recv.at[off], {"dp": peer}
        )

    def each_peer(action):
        def step(off, carry):
            action(off)
            return carry

        lax.fori_loop(1, group, step, 0)

    def earlier_of(own, store):
        return (
            dot(pick(positions, positions, -dilation), own)
            + dot(pick(positions, halo, halo - dilation), store)
        ).astype(jnp.bfloat16)

    def later_of(own, store):
        return (
            dot(pick(positions, positions, dilation), own)
            + dot(pick(positions, halo, dilation - positions), store)
        ).astype(jnp.bfloat16)

    def forward(m, carry):
        @pl.when(first)
        def _():
            h_in[m] = inputs[m]

        @pl.when(jnp.logical_not(first))
        def _():
            forward_copy(m).wait_recv()

        unit, _unused = normed(h_in[m].astype(jnp.float32))
        own = gelu(unit * gain_conv[...]).astype(jnp.bfloat16)
        columns[m, :, channels : 2 * channels] = own
        start_halos(0, m)
        total = dot(own, w_conv[channels : 2 * channels])
        wait_halos(0, m)
        earlier = earlier_of(own, halo_a[m, 0])
        columns[m, :, :channels] = earlier
        total = total + dot(earlier, w_conv[:channels])
        later = later_of(own, halo_a[m, 1])
        columns[m, :, 2 * channels :] = later
        total = total + dot(later, w_conv[2 * channels :])
        conv[m] = total
        unit, _unused = normed(total)
        mixture = gelu(unit * gain_point[...]).astype(jnp.bfloat16)
        mix[m] = mixture

        @pl.when(jnp.logical_not(last))
        def _():
            branch = dot(mix[m], w_point[...])
            h_out[m] = (h_in[m].astype(jnp.float32) + branch).astype(jnp.bfloat16)
            forward_copy(m).start()

        each_peer(lambda off: acts_copy(m, off).start())
        return carry

    lax.fori_loop(0, micros, forward, 0)

    def backward(m, carry):
        @pl.when(last)
        def _():
            e_in[m] = grad_out[m]

        @pl.when(jnp.logical_not(last))
        def _():
            backward_copy(m).wait_recv()

        grad_mix = dot_nt(e_in[m], w_point[...])
        grad_conv, grad_gain = act_pull(conv[m], gain_point[...], grad_mix)
        gains[:, channels:] += grad_gain
        own = grad_conv.astype(jnp.bfloat16)
        q_own[m] = own
        start_halos(1, m)
        back = dot_nt(own, w_conv[channels : 2 * channels])
        wait_halos(1, m)
        back = back + dot_nt(later_of(own, halo_q[m, 1]), w_conv[:channels])
        back = back + dot_nt(earlier_of(own, halo_q[m, 0]), w_conv[2 * channels :])
        grad_in, grad_gain = act_pull(h_in[m].astype(jnp.float32), gain_conv[...], back)
        gains[:, :channels] += grad_gain
        grads[m] = (e_in[m].astype(jnp.float32) + grad_in).astype(jnp.bfloat16)

        @pl.when(jnp.logical_not(first))
        def _():
            backward_copy(m).start()

        each_peer(lambda off: q_copy(m, off).start())
        point_sum[...] += dot_tn(mix[m], e_in[m])
        return carry

    lax.fori_loop(0, micros, backward, 0)

    rows = inner // group
    for owner in range(group):
        point_own[owner] = point_sum[owner * rows : (owner + 1) * rows].astype(jnp.bfloat16)
    each_peer(lambda off: gains_copy(off).start())
    each_peer(lambda off: point_copy(off).start())

    own_copies = [
        pltpu.make_async_copy(point_own.at[me], point_all.at[me], own_sem.at[0]),
        pltpu.make_async_copy(gains, gains_all.at[me], own_sem.at[1]),
    ]
    for m in range(micros):
        own_copies += [
            pltpu.make_async_copy(acts_part(m, me), acts_all.at[me, m], own_sem.at[2 + 2 * m]),
            pltpu.make_async_copy(q_own.at[m], q_all.at[me, m], own_sem.at[3 + 2 * m]),
        ]
    for copy in own_copies:
        copy.start()
    for copy in own_copies:
        copy.wait()

    def finish(m, carry):
        for kind in range(2):
            wait_halo_sends(kind, m)

        @pl.when(jnp.logical_not(last))
        def _():
            forward_copy(m).wait_send()

        @pl.when(jnp.logical_not(first))
        def _():
            backward_copy(m).wait_send()

        each_peer(lambda off: acts_copy(m, off).wait())
        each_peer(lambda off: q_copy(m, off).wait())
        return carry

    lax.fori_loop(0, micros, finish, 0)
    each_peer(lambda off: gains_copy(off).wait())
    each_peer(lambda off: point_copy(off).wait())


def on_device(inputs, grad_out, w_conv, w_point, gain_conv, gain_point):
    micros, positions, channels = inputs.shape
    sections, group = lax.axis_size("section"), lax.axis_size("dp")
    me = lax.axis_index("dp")
    inner = w_conv.shape[2]
    norm_scale = 1.0 / math.sqrt(micros * positions * group)
    reach = 3 ** (sections - 1) // 2 ** (sections - 1)
    halo = -(-reach // 16) * 16
    share, rows = 3 * channels // group, inner // group
    wide = window(share)
    bf16, f32 = jnp.bfloat16, jnp.float32
    dma = pltpu.SemaphoreType.DMA
    vmem = pl.BlockSpec(memory_space=pltpu.VMEM)
    anywhere = pl.BlockSpec(memory_space=pl.ANY)
    with jax.named_scope("tower"):
        grads, acts_all, q_all, point_all, gains_all = pl.pallas_call(
            functools.partial(tower, sections, group, halo),
            out_shape=[
                jax.ShapeDtypeStruct(inputs.shape, bf16),
                jax.ShapeDtypeStruct((group, micros, positions, wide), bf16),
                jax.ShapeDtypeStruct((group, micros, positions, inner), bf16),
                jax.ShapeDtypeStruct((group, rows, channels), bf16),
                jax.ShapeDtypeStruct((group, 1, channels + inner), f32),
            ],
            in_specs=[vmem] * 6,
            out_specs=[vmem] + [anywhere] * 4,
            scratch_shapes=[
                pltpu.VMEM((micros, positions, channels), bf16),
                pltpu.VMEM((micros, positions, channels), bf16),
                pltpu.VMEM((micros, positions, channels), bf16),
                pltpu.VMEM((micros, positions, inner), f32),
                pltpu.VMEM((micros, positions, inner), bf16),
                pltpu.VMEM((micros, positions, 3 * channels), bf16),
                pltpu.VMEM((micros, positions, inner), bf16),
                pltpu.VMEM((micros, 2, halo, channels), bf16),
                pltpu.VMEM((micros, 2, halo, inner), bf16),
                pltpu.VMEM((inner, channels), f32),
                pltpu.VMEM((group, rows, channels), bf16),
                pltpu.VMEM((1, channels + inner), f32),
                dma((2, micros)), dma((2, micros)),
                dma((2, micros, 2)), dma((2, micros, 2)),
                dma((micros, group)), dma((micros, group)),
                dma((micros, group)), dma((micros, group)),
                dma((group,)), dma((group,)),
                dma((group,)), dma((group,)),
                dma((2 + 2 * micros,)),
            ],
            compiler_params=pltpu.CompilerParams(
                collective_id=0, has_side_effects=True, vmem_limit_bytes=56 * 2**20
            ),
        )(inputs, grad_out, w_conv[0], w_point[0], gain_conv, gain_point)

    total = group * micros * positions
    conv_rows = lax.dot_general(
        acts_all.reshape(total, wide), q_all.reshape(total, inner),
        (((0,), (0,)), ((), ())), preferred_element_type=f32,
    )
    share_conv = lax.dynamic_slice_in_dim(conv_rows, lax.rem(share * me, 128), share, 0)
    share_point = jnp.sum(point_all.astype(f32), axis=0)
    gains = jnp.sum(gains_all, axis=(0, 1))
    own_c, own_p = channels // group, inner // group
    share_gc = lax.dynamic_slice_in_dim(gains, me * own_c, own_c, 0)
    share_gp = lax.dynamic_slice_in_dim(gains, channels + me * own_p, own_p, 0)
    return (
        (share_conv * norm_scale)[None],
        (share_point * norm_scale)[None],
        (share_gc * norm_scale)[None],
        (share_gp * norm_scale)[None],
        grads[None],
    )


def solution(mesh):
    return jax.shard_map(
        on_device,
        mesh=mesh,
        in_specs=(
            P(None, "dp", None),
            P(None, "dp", None),
            P("section", None, None),
            P("section", None, None),
            P("section", None),
            P("section", None),
        ),
        out_specs=(
            P("section", "dp", None),
            P("section", "dp", None),
            P("section", "dp"),
            P("section", "dp"),
            P("section", None, "dp", None),
        ),
        check_vma=False,
    )
```

profile of v0, /device:TPU:24, one launch (start us, length us, event | category | flops | bytes accessed | tf_op | source)
XLA Modules:
  0.0 302.9 jit_solution(13588407718662604951)
XLA Ops:
  0.6 291.6 %tower.1 = (bf16[2,128,1536]{2,1,0:T(8,128)(2,1)}, bf16[8,2,128,640]{3,2,1,0:T(8,128)(2,1)}, bf16[8,2,128,768]{3,2,1,0:T(8,128)(2,1)}, bf16[8,96,1536]{2,1,0:T(8,128)(2,1)}, f32[8,1,2304]{2,1,0:T(1,128)}) custom-call(bf16[2,128,1536]{2,1,0:T(8,128)(2,1)} %inputs.1, bf16[2,128,1536]{2,1,0:T(8,128)(2,1)} %grad_out.1, bf16[4608,768]{1,0:T(8,128)(2,1)} %bitcast.16, ...), custom_call_target="tpu_custom_call" | custom-call | tf_op jit(solution)/shard_map/tower/pallas_call | solution.py:344
  292.2 4.9 %convolution_bitcast_fusion = f32[640,768]{1,0:T(8,128)S(1)} fusion(bf16[8,2,128,640]{3,2,1,0:T(8,128)(2,1)} %get-tuple-element.10, bf16[8,2,128,768]{3,2,1,0:T(8,128)(2,1)} %get-tuple-element.11), kind=kOutput, calls=%fused_computation.2 | convolution fusion | flops 2013265920 | bytes 7733248 | tf_op jit(solution)/shard_map/dot_general | solution.py:382
  297.2 0.0 copy-start
  297.2 1.4 multiply_bitcast_fusion
  298.6 0.0 copy-start.2
  298.6 0.0 copy-start.1
  298.6 0.9 copy-done
  299.5 0.3 convert_reduce_fusion
  299.8 0.9 multiply_bitcast_fusion.1
  300.7 0.0 copy-done.2
  300.7 0.1 reduce_sum.19
  300.8 0.6 dynamic-slice_multiply_fusion
  301.4 0.6 multiply_bitcast_fusion.2
  302.0 0.0 copy-done.1
  302.0 0.9 copy.15
Async XLA Ops:
  297.2 2.3 copy-start
  298.6 2.1 copy-start.2
  298.6 3.4 %copy-start.1 = (bf16[2,128,1536]{2,1,0:T(8,128)(2,1)S(1)}, bf16[2,128,1536]{2,1,0:T(8,128)(2,1)}, u32[]{:S(2)}) copy-start(bf16[2,128,1536]{2,1,0:T(8,128)(2,1)} %get-tuple-element.14) | copy-start | bytes 2359300
where the time goes:
time: 305 us; the launch traced here: 303 us
  Pallas kernels  292 us (96%)
  matrix products  4.93 us (2%)
  other arithmetic  3.84 us (1%)
    pallas_call x1, Pallas kernels, on_device(): pl.pallas_call(functools.partial(tower, sections, group, halo), out_shape...  292 us

commit v1 on v0

--- a/solution.py
+++ b/solution.py
@@ -69,9 +69,11 @@
     sections, group, halo,
     inputs, grad_out, w_conv, w_point, gain_conv, gain_point,
     grads, acts_all, q_all, point_all, gains_all,
-    h_in, h_out, e_in, conv, mix, columns, q_own, halo_a, halo_q, point_sum, point_own, gains,
+    h_in, h_out, e_in, conv, mix, columns, q_own, halo_a, halo_q, point_sum, pair_out, pair_in,
+    point_out, gains,
     sec_send, sec_recv, halo_send, halo_recv,
-    acts_send, acts_recv, q_send, q_recv, point_send, point_recv, gains_send, gains_recv, own_sem,
+    acts_send, acts_recv, q_send, q_recv, pass_send, pass_recv, pair_send, pair_recv,
+    point_send, point_recv, gains_send, gains_recv, own_sem,
 ):
     section = lax.axis_index("section")
     me = lax.axis_index("dp")
@@ -81,6 +83,10 @@
     wide = window(share)
     first, last = section == 0, section == sections - 1
     left_end, right_end = me == 0, me == group - 1
+    half = group // 2
+    parity, spot = lax.rem(me, 2), me // 2
+    partner = me + 1 - 2 * parity
+    rows = inner // group
 
     dilation = jnp.int32(1)
     for index in range(sections):
@@ -177,17 +183,37 @@
             {"dp": peer},
         )
 
+    def column_peer(off):
+        return 2 * lax.rem(spot + off, half) + parity
+
     def q_copy(m, off):
-        peer = lax.rem(me + off, group)
-        return remote(
-            q_own.at[m], q_all.at[me, m], q_send.at[m, off], q_recv.at[m, off], {"dp": peer}
+        return remote(
+            q_own.at[m], q_all.at[me, m], q_send.at[m, off], q_recv.at[m, off],
+            {"dp": column_peer(off)},
+        )
+
+    def pass_copy(m, off):
+        source = 2 * lax.rem(spot - off + half, half) + parity
+        return remote(
+            q_all.at[source, m], q_all.at[source, m], pass_send.at[m, off], pass_recv.at[m, off],
+            {"dp": partner},
+        )
+
+    def own_pass_copy(m):
+        return remote(
+            q_own.at[m], q_all.at[me, m], pass_send.at[m, 0], pass_recv.at[m, 0],
+            {"dp": partner},
+        )
+
+    def pair_copy(i):
+        return remote(
+            pair_out.at[i], pair_in.at[i], pair_send.at[i], pair_recv.at[i], {"dp": partner}
         )
 
     def point_copy(off):
-        peer = lax.rem(me + off, group)
-        return remote(
-            point_own.at[peer], point_all.at[me], point_send.at[off], point_recv.at[off],
-            {"dp": peer},
+        return remote(
+            point_out.at[lax.rem(spot + off, half)], point_all.at[spot],
+            point_send.at[off], point_recv.at[off], {"dp": column_peer(off)},
         )
 
     def gains_copy(off):
@@ -202,6 +228,27 @@
             return carry
 
         lax.fori_loop(1, group, step, 0)
+
+    def each_column_peer(action):
+        def step(off, carry):
+            action(off)
+            return carry
+
+        lax.fori_loop(1, half, step, 0)
+
+    def pass_on(m):
+        def step(off):
+            q_copy(m, off).wait_recv()
+            pass_copy(m, off).start()
+
+        each_column_peer(step)
+
+    def start_acts():
+        def step(m, carry):
+            each_peer(lambda off: acts_copy(m, off).start())
+            return carry
+
+        lax.fori_loop(0, micros, step, 0)
 
     def earlier_of(own, store):
         return (
@@ -247,10 +294,13 @@
             h_out[m] = (h_in[m].astype(jnp.float32) + branch).astype(jnp.bfloat16)
             forward_copy(m).start()
 
-        each_peer(lambda off: acts_copy(m, off).start())
         return carry
 
     lax.fori_loop(0, micros, forward, 0)
+
+    @pl.when(jnp.logical_not(last))
+    def _():
+        start_acts()
 
     def backward(m, carry):
         @pl.when(last)
@@ -279,20 +329,45 @@
         def _():
             backward_copy(m).start()
 
-        each_peer(lambda off: q_copy(m, off).start())
+        each_column_peer(lambda off: q_copy(m, off).start())
+        own_pass_copy(m).start()
+
+        @pl.when(m > 0)
+        def _():
+            pass_on(m - 1)
+
         point_sum[...] += dot_tn(mix[m], e_in[m])
         return carry
 
     lax.fori_loop(0, micros, backward, 0)
 
-    rows = inner // group
-    for owner in range(group):
-        point_own[owner] = point_sum[owner * rows : (owner + 1) * rows].astype(jnp.bfloat16)
+    def block(i, side):
+        start = pl.multiple_of((2 * i + side) * rows, 8)
+        return point_sum[pl.ds(start, rows), :]
+
+    def send_pair(i, carry):
+        pair_out[i] = block(i, 1 - parity).astype(jnp.bfloat16)
+        pair_copy(i).start()
+        return carry
+
+    lax.fori_loop(0, half, send_pair, 0)
     each_peer(lambda off: gains_copy(off).start())
-    each_peer(lambda off: point_copy(off).start())
+    pass_on(micros - 1)
+
+    def add_pair(i, carry):
+        pair_copy(i).wait_recv()
+        point_out[i] = (block(i, parity) + pair_in[i].astype(jnp.float32)).astype(jnp.bfloat16)
+        return carry
+
+    lax.fori_loop(0, half, add_pair, 0)
+    each_column_peer(lambda off: point_copy(off).start())
+
+    @pl.when(last)
+    def _():
+        start_acts()
 
     own_copies = [
-        pltpu.make_async_copy(point_own.at[me], point_all.at[me], own_sem.at[0]),
+        pltpu.make_async_copy(point_out.at[spot], point_all.at[spot], own_sem.at[0]),
         pltpu.make_async_copy(gains, gains_all.at[me], own_sem.at[1]),
     ]
     for m in range(micros):
@@ -318,12 +393,20 @@
             backward_copy(m).wait_send()
 
         each_peer(lambda off: acts_copy(m, off).wait())
-        each_peer(lambda off: q_copy(m, off).wait())
+        each_column_peer(lambda off: q_copy(m, off).wait_send())
+        own_pass_copy(m).wait()
+        each_column_peer(lambda off: pass_copy(m, off).wait())
         return carry
 
     lax.fori_loop(0, micros, finish, 0)
     each_peer(lambda off: gains_copy(off).wait())
-    each_peer(lambda off: point_copy(off).wait())
+    each_column_peer(lambda off: point_copy(off).wait())
+
+    def finish_pair(i, carry):
+        pair_copy(i).wait_send()
+        return carry
+
+    lax.fori_loop(0, half, finish_pair, 0)
 
 
 def on_device(inputs, grad_out, w_conv, w_point, gain_conv, gain_point):
@@ -336,6 +419,7 @@
     halo = -(-reach // 16) * 16
     share, rows = 3 * channels // group, inner // group
     wide = window(share)
+    half = group // 2
     bf16, f32 = jnp.bfloat16, jnp.float32
     dma = pltpu.SemaphoreType.DMA
     vmem = pl.BlockSpec(memory_space=pltpu.VMEM)
@@ -347,7 +431,7 @@
                 jax.ShapeDtypeStruct(inputs.shape, bf16),
                 jax.ShapeDtypeStruct((group, micros, positions, wide), bf16),
                 jax.ShapeDtypeStruct((group, micros, positions, inner), bf16),
-                jax.ShapeDtypeStruct((group, rows, channels), bf16),
+                jax.ShapeDtypeStruct((half, rows, channels), bf16),
                 jax.ShapeDtypeStruct((group, 1, channels + inner), f32),
             ],
             in_specs=[vmem] * 6,
@@ -363,13 +447,17 @@
                 pltpu.VMEM((micros, 2, halo, channels), bf16),
                 pltpu.VMEM((micros, 2, halo, inner), bf16),
                 pltpu.VMEM((inner, channels), f32),
-                pltpu.VMEM((group, rows, channels), bf16),
+                pltpu.VMEM((half, rows, channels), bf16),
+                pltpu.VMEM((half, rows, channels), bf16),
+                pltpu.VMEM((half, rows, channels), bf16),
                 pltpu.VMEM((1, channels + inner), f32),
                 dma((2, micros)), dma((2, micros)),
                 dma((2, micros, 2)), dma((2, micros, 2)),
                 dma((micros, group)), dma((micros, group)),
-                dma((micros, group)), dma((micros, group)),
-                dma((group,)), dma((group,)),
+                dma((micros, half)), dma((micros, half)),
+                dma((micros, half)), dma((micros, half)),
+                dma((half,)), dma((half,)),
+                dma((half,)), dma((half,)),
                 dma((group,)), dma((group,)),
                 dma((2 + 2 * micros,)),
             ],

time: 305 us -> 213 us (0.70)
  Pallas kernels: 292 us -> 202 us
    pallas_call x1, Pallas kernels: 292 us -> 202 us  [on_device(): pl.pallas_call(functools.partial(tower, sections, group, halo), out_shape...]
where the time goes in v1:
time: 213 us; the launch traced here: 212 us
  Pallas kernels  202 us (95%)
  matrix products  4.93 us (2%)
  other arithmetic  3.68 us (2%)
    pallas_call x1, Pallas kernels, on_device(): pl.pallas_call(functools.partial(tower, sections, group, halo), out_shape...  202 us
    dot_general x1, matrix products, on_device(): lax.dot_general(acts_all.reshape(total, wide), q_all.reshape(total, inner...  4.93 us

profile of v1, /device:TPU:24, one launch (start us, length us, event | category | flops | bytes accessed | tf_op | source)
XLA Modules:
  0.0 212.4 jit_solution(2677445794787401089)
XLA Ops:
  0.6 202.0 %tower.1 = (bf16[2,128,1536]{2,1,0:T(8,128)(2,1)}, bf16[8,2,128,640]{3,2,1,0:T(8,128)(2,1)}, bf16[8,2,128,768]{3,2,1,0:T(8,128)(2,1)}, bf16[4,96,1536]{2,1,0:T(8,128)(2,1)}, f32[8,1,2304]{2,1,0:T(1,128)}) custom-call(bf16[2,128,1536]{2,1,0:T(8,128)(2,1)} %inputs.1, bf16[2,128,1536]{2,1,0:T(8,128)(2,1)} %grad_out.1, bf16[4608,768]{1,0:T(8,128)(2,1)} %bitcast.16, ...), custom_call_target="tpu_custom_call" | custom-call | tf_op jit(solution)/shard_map/tower/pallas_call | solution.py:428
  202.6 4.9 %convolution_bitcast_fusion = f32[640,768]{1,0:T(8,128)S(1)} fusion(bf16[8,2,128,640]{3,2,1,0:T(8,128)(2,1)} %get-tuple-element.10, bf16[8,2,128,768]{3,2,1,0:T(8,128)(2,1)} %get-tuple-element.11), kind=kOutput, calls=%fused_computation.2 | convolution fusion | flops 2013265920 | bytes 7733248 | tf_op jit(solution)/shard_map/dot_general | solution.py:470
  207.6 0.0 copy-start
  207.6 1.4 multiply_bitcast_fusion
  208.9 0.0 copy-start.2
  208.9 0.0 copy-start.1
  208.9 0.3 copy-done
  209.2 0.2 convert_reduce_fusion
  209.4 0.9 multiply_bitcast_fusion.1
  210.3 0.0 copy-done.2
  210.3 0.1 reduce_sum.19
  210.3 0.6 dynamic-slice_multiply_fusion
  211.0 0.6 multiply_bitcast_fusion.2
  211.6 0.0 copy-done.1
  211.6 0.9 copy.15
Async XLA Ops:
  207.6 1.7 copy-start
  208.9 1.3 copy-start.2
  208.9 2.6 %copy-start.1 = (bf16[2,128,1536]{2,1,0:T(8,128)(2,1)S(1)}, bf16[2,128,1536]{2,1,0:T(8,128)(2,1)}, u32[]{:S(2)}) copy-start(bf16[2,128,1536]{2,1,0:T(8,128)(2,1)} %get-tuple-element.14) | copy-start | bytes 2359300

commit v2 on v1

--- a/solution.py
+++ b/solution.py
@@ -95,7 +95,6 @@
     halo_a[...] = jnp.zeros_like(halo_a)
     halo_q[...] = jnp.zeros_like(halo_q)
     gains[...] = jnp.zeros_like(gains)
-    point_sum[...] = jnp.zeros_like(point_sum)
 
     barrier = pltpu.get_barrier_semaphore()
 
@@ -115,8 +114,20 @@
     def _():
         pl.semaphore_signal(barrier, inc=1, device_id={"section": section + 1}, device_id_type=MESH)
 
+    def greet_diagonal(there, step, by):
+        @pl.when(jnp.logical_and(there, jnp.logical_not(left_end if step < 0 else right_end)))
+        def _():
+            pl.semaphore_signal(
+                barrier, inc=1, device_id={"section": section + by, "dp": me + step},
+                device_id_type=MESH,
+            )
+
+    for step in (-1, 1):
+        greet_diagonal(jnp.logical_not(first), step, -1)
+        greet_diagonal(jnp.logical_not(last), step, 1)
     beside = jnp.where(first, 0, 1) + jnp.where(last, 0, 1)
-    pl.semaphore_wait(barrier, group - 1 + beside)
+    ends = jnp.where(left_end, 0, 1) + jnp.where(right_end, 0, 1)
+    pl.semaphore_wait(barrier, group - 1 + beside * (1 + ends))
 
     def remote(src, dst, send, recv, device):
         return pltpu.make_async_remote_copy(
@@ -124,25 +135,31 @@
             device_id=device, device_id_type=MESH,
         )
 
-    def forward_copy(m):
-        return remote(
-            h_out.at[m], h_in.at[m], sec_send.at[0, m], sec_recv.at[0, m], {"section": section + 1}
+    def forward_copy(m, part):
+        place = pl.ds(part * (channels // 2), channels // 2)
+        return remote(
+            h_out.at[m, :, place], h_in.at[m, :, place],
+            sec_send.at[part, m], sec_recv.at[part, m], {"section": section + 1},
         )
 
     def backward_copy(m):
         return remote(
-            grads.at[m], e_in.at[m], sec_send.at[1, m], sec_recv.at[1, m], {"section": section - 1}
+            grads.at[m], e_in.at[m], sec_send.at[2, m], sec_recv.at[2, m], {"section": section - 1}
         )
 
     def halo_copy(kind, m, side):
         rows = pl.ds(positions - halo, halo) if side == 0 else pl.ds(0, halo)
+        device = {"dp": me + 1 if side == 0 else me - 1}
         if kind == 0:
-            src, store = columns.at[m, rows, pl.ds(channels, channels)], halo_a
+            src, store = h_out.at[m, rows], halo_a
+            device["section"] = section + 1
+        elif kind == 1:
+            src, store = q_own.at[m, rows], halo_q
         else:
-            src, store = q_own.at[m, rows], halo_q
-        return remote(
-            src, store.at[m, side], halo_send.at[kind, m, side], halo_recv.at[kind, m, side],
-            {"dp": me + 1 if side == 0 else me - 1},
+            src, store = inputs.at[m, rows], halo_a
+        return remote(
+            src, store.at[m, side], halo_send.at[kind, m, side], halo_recv.at[kind % 2, m, side],
+            device,
         )
 
     def start_halos(kind, m):
@@ -262,6 +279,11 @@
             + dot(pick(positions, halo, dilation - positions), store)
         ).astype(jnp.bfloat16)
 
+    @pl.when(first)
+    def _():
+        for m in range(micros):
+            start_halos(2, m)
+
     def forward(m, carry):
         @pl.when(first)
         def _():
@@ -269,18 +291,21 @@
 
         @pl.when(jnp.logical_not(first))
         def _():
-            forward_copy(m).wait_recv()
-
-        unit, _unused = normed(h_in[m].astype(jnp.float32))
-        own = gelu(unit * gain_conv[...]).astype(jnp.bfloat16)
+            for part in range(2):
+                forward_copy(m, part).wait_recv()
+
+        def activated(values):
+            unit, _unused = normed(values.astype(jnp.float32))
+            return gelu(unit * gain_conv[...]).astype(jnp.bfloat16)
+
+        own = activated(h_in[m])
         columns[m, :, channels : 2 * channels] = own
-        start_halos(0, m)
         total = dot(own, w_conv[channels : 2 * channels])
         wait_halos(0, m)
-        earlier = earlier_of(own, halo_a[m, 0])
+        earlier = earlier_of(own, activated(halo_a[m, 0]))
         columns[m, :, :channels] = earlier
         total = total + dot(earlier, w_conv[:channels])
-        later = later_of(own, halo_a[m, 1])
+        later = later_of(own, activated(halo_a[m, 1]))
         columns[m, :, 2 * channels :] = later
         total = total + dot(later, w_conv[2 * channels :])
         conv[m] = total
@@ -290,9 +315,14 @@
 
         @pl.when(jnp.logical_not(last))
         def _():
-            branch = dot(mix[m], w_point[...])
-            h_out[m] = (h_in[m].astype(jnp.float32) + branch).astype(jnp.bfloat16)
-            forward_copy(m).start()
+            for part in range(2):
+                place = slice(part * (channels // 2), (part + 1) * (channels // 2))
+                branch = dot(mix[m], w_point[:, place])
+                h_out[m, :, place] = (
+                    h_in[m, :, place].astype(jnp.float32) + branch
+                ).astype(jnp.bfloat16)
+                forward_copy(m, part).start()
+            start_halos(0, m)
 
         return carry
 
@@ -301,6 +331,20 @@
     @pl.when(jnp.logical_not(last))
     def _():
         start_acts()
+
+    def block(i, side):
+        start = pl.multiple_of((2 * i + side) * rows, 8)
+        return point_sum[pl.ds(start, rows), :]
+
+    def send_pair(i, carry):
+        pair_out[i] = block(i, 1 - parity).astype(jnp.bfloat16)
+        pair_copy(i).start()
+        return carry
+
+    def send_point():
+        every = micros * positions
+        point_sum[...] = dot_tn(mix[...].reshape(every, inner), e_in[...].reshape(every, channels))
+        lax.fori_loop(0, half, send_pair, 0)
 
     def backward(m, carry):
         @pl.when(last)
@@ -317,6 +361,13 @@
         own = grad_conv.astype(jnp.bfloat16)
         q_own[m] = own
         start_halos(1, m)
+        each_column_peer(lambda off: q_copy(m, off).start())
+        own_pass_copy(m).start()
+
+        @pl.when(jnp.logical_and(first, m == micros - 1))
+        def _():
+            send_point()
+
         back = dot_nt(own, w_conv[channels : 2 * channels])
         wait_halos(1, m)
         back = back + dot_nt(later_of(own, halo_q[m, 1]), w_conv[:channels])
@@ -329,28 +380,18 @@
         def _():
             backward_copy(m).start()
 
-        each_column_peer(lambda off: q_copy(m, off).start())
-        own_pass_copy(m).start()
-
         @pl.when(m > 0)
         def _():
             pass_on(m - 1)
 
-        point_sum[...] += dot_tn(mix[m], e_in[m])
         return carry
 
     lax.fori_loop(0, micros, backward, 0)
 
-    def block(i, side):
-        start = pl.multiple_of((2 * i + side) * rows, 8)
-        return point_sum[pl.ds(start, rows), :]
-
-    def send_pair(i, carry):
-        pair_out[i] = block(i, 1 - parity).astype(jnp.bfloat16)
-        pair_copy(i).start()
-        return carry
-
-    lax.fori_loop(0, half, send_pair, 0)
+    @pl.when(jnp.logical_not(first))
+    def _():
+        send_point()
+
     each_peer(lambda off: gains_copy(off).start())
     pass_on(micros - 1)
 
@@ -381,12 +422,17 @@
         copy.wait()
 
     def finish(m, carry):
-        for kind in range(2):
-            wait_halo_sends(kind, m)
+        wait_halo_sends(1, m)
+
+        @pl.when(first)
+        def _():
+            wait_halo_sends(2, m)
 
         @pl.when(jnp.logical_not(last))
         def _():
-            forward_copy(m).wait_send()
+            wait_halo_sends(0, m)
+            for part in range(2):
+                forward_copy(m, part).wait_send()
 
         @pl.when(jnp.logical_not(first))
         def _():
@@ -451,8 +497,8 @@
                 pltpu.VMEM((half, rows, channels), bf16),
                 pltpu.VMEM((half, rows, channels), bf16),
                 pltpu.VMEM((1, channels + inner), f32),
-                dma((2, micros)), dma((2, micros)),
-                dma((2, micros, 2)), dma((2, micros, 2)),
+                dma((3, micros)), dma((3, micros)),
+                dma((3, micros, 2)), dma((3, micros, 2)),
                 dma((micros, group)), dma((micros, group)),
                 dma((micros, half)), dma((micros, half)),
                 dma((micros, half)), dma((micros, half)),

time: 213 us -> 204 us (0.958)
  Pallas kernels: 202 us -> 192 us
    pallas_call x1, Pallas kernels: 202 us -> 192 us  [on_device(): pl.pallas_call(functools.partial(tower, sections, group, halo), out_shape...]
where the time goes in v2:
time: 204 us; the launch traced here: 202 us
  Pallas kernels  192 us (94%)
  matrix products  4.94 us (2%)
  other arithmetic  3.68 us (2%)
    pallas_call x1, Pallas kernels, on_device(): pl.pallas_call(functools.partial(tower, sections, group, halo), out_shape...  192 us
    dot_general x1, matrix products, on_device(): lax.dot_general(acts_all.reshape(total, wide), q_all.reshape(total, inner...  4.94 us

profile of v2, /device:TPU:24, one launch (start us, length us, event | category | flops | bytes accessed | tf_op | source)
XLA Modules:
  0.0 202.2 jit_solution(13125123164994491450)
XLA Ops:
  0.6 191.7 %tower.1 = (bf16[2,128,1536]{2,1,0:T(8,128)(2,1)}, bf16[8,2,128,640]{3,2,1,0:T(8,128)(2,1)}, bf16[8,2,128,768]{3,2,1,0:T(8,128)(2,1)}, bf16[4,96,1536]{2,1,0:T(8,128)(2,1)}, f32[8,1,2304]{2,1,0:T(1,128)}) custom-call(bf16[2,128,1536]{2,1,0:T(8,128)(2,1)} %inputs.1, bf16[2,128,1536]{2,1,0:T(8,128)(2,1)} %grad_out.1, bf16[4608,768]{1,0:T(8,128)(2,1)} %bitcast.16, ...), custom_call_target="tpu_custom_call" | custom-call | tf_op jit(solution)/shard_map/tower/pallas_call | solution.py:474
  192.4 4.9 %convolution_bitcast_fusion = f32[640,768]{1,0:T(8,128)S(1)} fusion(bf16[8,2,128,640]{3,2,1,0:T(8,128)(2,1)} %get-tuple-element.10, bf16[8,2,128,768]{3,2,1,0:T(8,128)(2,1)} %get-tuple-element.11), kind=kOutput, calls=%fused_computation.2 | convolution fusion | flops 2013265920 | bytes 7733248 | tf_op jit(solution)/shard_map/dot_general | solution.py:516
  197.3 0.0 copy-start
  197.3 1.4 multiply_bitcast_fusion
  198.7 0.0 copy-start.2
  198.7 0.0 copy-start.1
  198.7 0.3 copy-done
  199.0 0.2 convert_reduce_fusion
  199.2 0.9 multiply_bitcast_fusion.1
  200.0 0.0 copy-done.2
  200.0 0.1 reduce_sum.19
  200.1 0.6 dynamic-slice_multiply_fusion
  200.7 0.6 multiply_bitcast_fusion.2
  201.3 0.0 copy-done.1
  201.3 0.9 copy.15
Async XLA Ops:
  197.3 1.7 copy-start
  198.7 1.3 copy-start.2
  198.7 2.6 %copy-start.1 = (bf16[2,128,1536]{2,1,0:T(8,128)(2,1)S(1)}, bf16[2,128,1536]{2,1,0:T(8,128)(2,1)}, u32[]{:S(2)}) copy-start(bf16[2,128,1536]{2,1,0:T(8,128)(2,1)} %get-tuple-element.14) | copy-start | bytes 2359300

commit v3 on v2

--- a/solution.py
+++ b/solution.py
@@ -68,8 +68,8 @@
 def tower(
     sections, group, halo,
     inputs, grad_out, w_conv, w_point, gain_conv, gain_point,
-    grads, acts_all, q_all, point_all, gains_all,
-    h_in, h_out, e_in, conv, mix, columns, q_own, halo_a, halo_q, point_sum, pair_out, pair_in,
+    grads, conv_rows, point_all, gains_all,
+    acts_all, q_all, h_in, h_out, e_in, conv, mix, columns, q_own, halo_a, halo_q, point_sum, pair_out, pair_in,
     point_out, gains,
     sec_send, sec_recv, halo_send, halo_recv,
     acts_send, acts_recv, q_send, q_recv, pass_send, pass_recv, pair_send, pair_recv,
@@ -328,7 +328,9 @@
 
     lax.fori_loop(0, micros, forward, 0)
 
-    @pl.when(jnp.logical_not(last))
+    early = section < sections // 2
+
+    @pl.when(early)
     def _():
         start_acts()
 
@@ -403,7 +405,7 @@
     lax.fori_loop(0, half, add_pair, 0)
     each_column_peer(lambda off: point_copy(off).start())
 
-    @pl.when(last)
+    @pl.when(jnp.logical_not(early))
     def _():
         start_acts()
 
@@ -421,6 +423,8 @@
     for copy in own_copies:
         copy.wait()
 
+    conv_rows[...] = jnp.zeros_like(conv_rows)
+
     def finish(m, carry):
         wait_halo_sends(1, m)
 
@@ -442,6 +446,15 @@
         each_column_peer(lambda off: q_copy(m, off).wait_send())
         own_pass_copy(m).wait()
         each_column_peer(lambda off: pass_copy(m, off).wait())
+
+        def contract(pair, inner_carry):
+            both = pl.ds(2 * pair, 2)
+            left = acts_all[both, m].reshape(2 * positions, wide)
+            right = q_all[both, m].reshape(2 * positions, inner)
+            conv_rows[...] += dot_tn(left, right)
+            return inner_carry
+
+        lax.fori_loop(0, half, contract, 0)
         return carry
 
     lax.fori_loop(0, micros, finish, 0)
@@ -471,18 +484,19 @@
     vmem = pl.BlockSpec(memory_space=pltpu.VMEM)
     anywhere = pl.BlockSpec(memory_space=pl.ANY)
     with jax.named_scope("tower"):
-        grads, acts_all, q_all, point_all, gains_all = pl.pallas_call(
+        grads, conv_rows, point_all, gains_all = pl.pallas_call(
             functools.partial(tower, sections, group, halo),
             out_shape=[
                 jax.ShapeDtypeStruct(inputs.shape, bf16),
-                jax.ShapeDtypeStruct((group, micros, positions, wide), bf16),
-                jax.ShapeDtypeStruct((group, micros, positions, inner), bf16),
+                jax.ShapeDtypeStruct((wide, inner), f32),
                 jax.ShapeDtypeStruct((half, rows, channels), bf16),
                 jax.ShapeDtypeStruct((group, 1, channels + inner), f32),
             ],
             in_specs=[vmem] * 6,
-            out_specs=[vmem] + [anywhere] * 4,
+            out_specs=[vmem] * 2 + [anywhere] * 2,
             scratch_shapes=[
+                pltpu.VMEM((group, micros, positions, wide), bf16),
+                pltpu.VMEM((group, micros, positions, inner), bf16),
                 pltpu.VMEM((micros, positions, channels), bf16),
                 pltpu.VMEM((micros, positions, channels), bf16),
                 pltpu.VMEM((micros, positions, channels), bf16),
@@ -512,11 +526,6 @@
             ),
         )(inputs, grad_out, w_conv[0], w_point[0], gain_conv, gain_point)
 
-    total = group * micros * positions
-    conv_rows = lax.dot_general(
-        acts_all.reshape(total, wide), q_all.reshape(total, inner),
-        (((0,), (0,)), ((), ())), preferred_element_type=f32,
-    )
     share_conv = lax.dynamic_slice_in_dim(conv_rows, lax.rem(share * me, 128), share, 0)
     share_point = jnp.sum(point_all.astype(f32), axis=0)
     gains = jnp.sum(gains_all, axis=(0, 1))

time: 204 us -> 191 us (0.936)
  the two profiles are of different devices: /device:TPU:24 before, /device:TPU:30 now
where the time goes in v3:
time: 191 us
  Pallas kernels  184 us (96%)
  other arithmetic  5.26 us (3%)
    pallas_call x1, Pallas kernels, on_device(): pl.pallas_call(functools.partial(tower, sections, group, halo), out_shape...  184 us

profile of v3, /device:TPU:30, one launch (start us, length us, event | category | flops | bytes accessed | tf_op | source)
XLA Modules:
  0.0 191.2 jit_solution(8784138651874302132)
XLA Ops:
  0.6 184.4 %tower.1 = (bf16[2,128,1536]{2,1,0:T(8,128)(2,1)}, f32[640,768]{1,0:T(8,128)}, bf16[4,96,1536]{2,1,0:T(8,128)(2,1)}, f32[8,1,2304]{2,1,0:T(1,128)}) custom-call(bf16[2,128,1536]{2,1,0:T(8,128)(2,1)} %inputs.1, bf16[2,128,1536]{2,1,0:T(8,128)(2,1)} %grad_out.1, bf16[4608,768]{1,0:T(8,128)(2,1)} %bitcast.10, bf16[768,1536]{1,0:T(8,128)(2,1)} %bitcast.11, ...), custom_call_target="tpu_custom_call" | custom-call | tf_op jit(solution)/shard_map/tower/pallas_call | solution.py:487
  185.0 0.0 copy-start.2
  185.1 0.0 copy-start
  185.1 2.9 %multiply_bitcast_fusion = f32[1,576,768]{2,1,0:T(8,128)} fusion(f32[640,768]{1,0:T(8,128)} %get-tuple-element.9, s32[]{:T(128)S(6)} %select_n.9), kind=kLoop, calls=%fused_computation.1 | loop fusion | flops 442368 | bytes 3538948 | tf_op jit(solution)/shard_map/broadcast_in_dim | solution.py:536
  188.0 0.0 copy-start.1
  188.0 0.0 copy-done.2
  188.0 0.1 reduce_sum.19
  188.1 0.6 dynamic-slice_multiply_fusion
  188.7 0.6 multiply_bitcast_fusion.2
  189.3 0.0 copy-done
  189.3 0.2 convert_reduce_fusion
  189.5 0.9 multiply_bitcast_fusion.1
  190.3 0.0 copy-done.1
  190.3 0.9 copy.12
Async XLA Ops:
  185.0 3.0 %copy-start.2 = (f32[8,1,2304]{2,1,0:T(1,128)S(1)}, f32[8,1,2304]{2,1,0:T(1,128)}, u32[]{:S(2)}) copy-start(f32[8,1,2304]{2,1,0:T(1,128)} %get-tuple-element.11) | copy-start | bytes 221188
  185.1 4.3 %copy-start = (bf16[4,96,1536]{2,1,0:T(8,128)(2,1)S(1)}, bf16[4,96,1536]{2,1,0:T(8,128)(2,1)}, u32[]{:S(2)}) copy-start(bf16[4,96,1536]{2,1,0:T(8,128)(2,1)} %get-tuple-element.10) | copy-start | bytes 3538948
  188.0 2.3 %copy-start.1 = (bf16[2,128,1536]{2,1,0:T(8,128)(2,1)S(1)}, bf16[2,128,1536]{2,1,0:T(8,128)(2,1)}, u32[]{:S(2)}) copy-start(bf16[2,128,1536]{2,1,0:T(8,128)(2,1)} %get-tuple-element.12) | copy-start | bytes 2359300
